TPU v7x, 256 devices: a whole 4x4x8 slice. The times are simulated.
256 devices in a mesh: seg: 64 (over x, z, core), sub: 4 (over y).
Axes of the slice: x: 4, y: 4, z: 8, core: 2. Of those that a mesh axis runs over, the one named last changes fastest.
Arguments:
- rhs_local: float32 [64, 4, 16, 32, 128], P('seg', 'sub'), may hold values from -6 to 6
- diag_inv: float32 [64, 4, 16, 128, 128], P('seg', 'sub')
- off_blocks: float32 [64, 4, 16, 4, 128, 128], P('seg', 'sub'), may hold values from -0.08 to 0.08
- pattern: int32 [64, 4, 16, 4], P('seg', 'sub'), may hold values from -1 to 17, as said below
- sep_rhs: float32 [64, 32, 128], P('seg'), may hold values from -6 to 6
- sep_inv: float32 [64, 128, 128], P('seg')
- coupling: float32 [64, 128, 128], P('seg'), may hold values from -0.4375 to 0.4375
Outputs:
- tree_solution: float32 [64, 4, 16, 32, 128], P('seg', 'sub')
- sep_solution: float32 [64, 32, 128], P('seg')
Inputs may be any that keep to these rules, and one draw needn't show every extreme that they name: In each row pattern[s, u, j], every entry is -1 (empty slot) or a target greater than j, and the filled targets of one row are distinct.
All inputs are finite; a program needn't handle non-finite values.
Results may differ from a plain program's by a relative error of at most 0.0003.
Values sent between devices are 32-bit elements; how exact they have to be, the bound alone decides.
A program may use at most 64 MiB of HBM per device.

v0:
```python
import jax
import jax.numpy as jnp
from jax import lax
from jax.sharding import PartitionSpec as P

HIGH = lax.Precision.HIGHEST


def passed_along(array, axis, by):
    count = lax.axis_size(axis)
    pairs = [(i, i + by) for i in range(count) if 0 <= i + by < count]
    return lax.ppermute(array, axis, pairs)


def tree_down(source, inverse, blocks, targets):
    supernodes = source.shape[0]
    updates = jnp.zeros((supernodes + 2,) + source.shape[1:], jnp.float32)
    solved = jnp.zeros_like(source)

    def tree_advance(position, state_pair):
        solved, updates = state_pair
        remain = source[position] - updates[position]
        column = jnp.einsum("rb,ab->ra", remain, inverse[position], precision=HIGH)
        products = jnp.einsum("rc,kac->kra", column, blocks[position], precision=HIGH)
        row_targets = targets[position]
        for slot_number in range(row_targets.shape[0]):
            target = jnp.maximum(row_targets[slot_number], 0)
            weight_on = (row_targets[slot_number] >= 0).astype(products.dtype)
            current = lax.dynamic_index_in_dim(updates, target, 0, keepdims=False)
            updates = lax.dynamic_update_index_in_dim(
                updates, current + weight_on * products[slot_number], target, 0
            )
        solved = lax.dynamic_update_index_in_dim(solved, column, position, 0)
        return (solved, updates)

    solved, updates = lax.fori_loop(0, supernodes, tree_advance, (solved, updates))
    return (solved, updates[supernodes], updates[supernodes + 1])


def tree_up(solved, inverse, blocks, targets, own_sep, left_sep):
    supernodes = solved.shape[0]
    known_rows = jnp.concatenate([jnp.zeros_like(solved), own_sep[None], left_sep[None]], 0)

    def retreat(offset, known_rows):
        position = supernodes - 1 - offset
        row_targets = targets[position]
        weight_on = (row_targets >= 0).astype(known_rows.dtype)[:, None, None]
        picked = known_rows[jnp.maximum(row_targets, 0)] * weight_on
        pulled = jnp.einsum("kra,kac->rc", picked, blocks[position], precision=HIGH)
        column = jnp.einsum(
            "ra,ac->rc", solved[position] - pulled, inverse[position], precision=HIGH
        )
        return lax.dynamic_update_index_in_dim(known_rows, column, position, 0)

    known_rows = lax.fori_loop(0, supernodes, retreat, known_rows)
    return known_rows[:supernodes]


def walk_chain(maps_all, offsets_all, backwards):

    def walk_advance(previous, pair):
        current = jnp.dot(previous, pair[0], precision=HIGH) + pair[1]
        return (current, current)

    _, states = lax.scan(
        walk_advance, jnp.zeros_like(offsets_all[0]), (maps_all, offsets_all), reverse=backwards
    )
    return states


def shards(rhs_local, diag_inv, off_blocks, pattern, sep_rhs, sep_inv, coupling):
    source = rhs_local[0, 0]
    inverse = diag_inv[0, 0]
    blocks = off_blocks[0, 0]
    targets = pattern[0, 0]
    sep_inverse = sep_inv[0]
    link_block = coupling[0]
    tree_forward, own_term, left_term = tree_down(source, inverse, blocks, targets)
    own_total, left_total = lax.psum((own_term, left_term), "sub")
    left_next, link_next = passed_along((left_total, link_block), "seg", -1)
    reduced = sep_rhs[0] - own_total - left_next
    offset_down = jnp.einsum("rb,ab->ra", reduced, sep_inverse, precision=HIGH)
    map_down = -jnp.einsum("kb,ak->ba", link_block, sep_inverse, precision=HIGH)
    maps_all, offsets_all = (
        lax.all_gather(map_down[None], "seg", axis=0, tiled=True),
        lax.all_gather(offset_down[None], "seg", axis=0, tiled=True),
    )
    forward_all = walk_chain(maps_all, offsets_all, False)
    position = lax.axis_index("seg")
    sep_forward = lax.dynamic_index_in_dim(forward_all, position, 0, keepdims=False)
    offset_up = jnp.dot(sep_forward, sep_inverse, precision=HIGH)
    map_up = -jnp.dot(link_next, sep_inverse, precision=HIGH)
    maps_back, offsets_back = (
        lax.all_gather(map_up[None], "seg", axis=0, tiled=True),
        lax.all_gather(offset_up[None], "seg", axis=0, tiled=True),
    )
    backward_all = walk_chain(maps_back, offsets_back, True)
    sep_solution = lax.dynamic_index_in_dim(backward_all, position, 0, keepdims=False)
    earlier = jnp.maximum(position - 1, 0)
    present = (position > 0).astype(jnp.float32)
    left_solution = lax.dynamic_index_in_dim(backward_all, earlier, 0, keepdims=False) * present
    tree_solution = tree_up(tree_forward, inverse, blocks, targets, sep_solution, left_solution)
    return (tree_solution[None, None], sep_solution[None])


def solution(mesh):
    in_specs = (
        P("seg", "sub", None, None, None),
        P("seg", "sub", None, None, None),
        P("seg", "sub", None, None, None, None),
        P("seg", "sub", None, None),
        P("seg", None, None),
        P("seg", None, None),
        P("seg", None, None),
    )
    out_specs = (P("seg", "sub", None, None, None), P("seg", None, None))
    return jax.shard_map(shards, mesh=mesh, in_specs=in_specs, out_specs=out_specs, check_vma=False)
```

profile of v0, /device:TPU:1, one launch (start us, length us, event | category | flops | bytes accessed | tf_op | source)
XLA Modules:
  0.0 611.3 jit_solution(7371041106820131612)
XLA Ops:
  7.3 144.8 %while.60 = (s32[]{:T(128)}, f32[16,32,128]{2,1,0:T(8,128)S(1)}, f32[18,32,128]{2,1,0:T(8,128)S(1)}, f32[16,32,128]{2,1,0:T(8,128)}, f32[16,128,128]{2,1,0:T(8,1...) while((s32[]{:T(128)}, f32[16,32,128]{2,1,0:T(8,128)S(1)}, ...), condition=%wide.region_1.2_spmd, body=%wide.region_0.1_spmd.sunk | while | flops 31494148 | bytes 674089 | solution.py:36
  11.1 1.4 convolution_bitcast_fusion.6
  20.2 1.4 convolution_bitcast_fusion.6
  38.3 1.4 convolution_bitcast_fusion.6
  47.3 1.4 convolution_bitcast_fusion.6
  65.4 1.4 convolution_bitcast_fusion.6
  74.5 1.4 convolution_bitcast_fusion.6
  92.6 1.4 convolution_bitcast_fusion.6
  101.6 1.4 convolution_bitcast_fusion.6
  119.7 1.4 convolution_bitcast_fusion.6
  128.7 1.4 convolution_bitcast_fusion.6
  146.8 1.4 convolution_bitcast_fusion.6
  152.1 14.4 %all-reduce = (f32[32,128]{1,0:T(8,128)S(1)}, f32[32,128]{1,0:T(8,128)S(1)}) all-reduce(f32[32,128]{1,0:T(8,128)S(1)} %get-tuple-element.520, f32[32,128]{1,0:T(8,128)S(1)} %get-tuple-element.519), channel_id=1, replica_groups=mesh['seg'=64,'sub'=4] {'sub'}, use_global_device_ids=true, to_apply=%region_3.4 | all-reduce | flops 8192 | bytes 65536 | tf_op jit(solution)/shard_map/psum | solution.py:79
  166.5 6.3 %collective-permute-start.1 = (f32[32,128]{1,0:T(8,128)S(1)}, f32[32,128]{1,0:T(8,128)S(1)}, u32[]{:S(2)}, u32[]{:S(2)}) collective-permute-start(f32[32,128]{1,0:T(8,128)S(1)} %get-tuple-element.505), channel_id=1, source_target_pairs={{4,0},{8,4},{12,8},{16,12},{20,16},{24,20},{28,24},{32,28},{36,32}... | collective-permute-start | bytes 49160 | tf_op jit(solution)/shard_map/ppermute | solution.py:12
  172.8 2.9 collective-permute-done.1
  177.7 1.9 collective-permute-start
  179.6 3.6 collective-permute-done
  184.2 69.2 %all-gather.13.cloned.1.call-done = f32[2048,128]{1,0:T(8,128)} async-done(((f32[32,128]{1,0:T(8,128)}), f32[2048,128]{1,0:T(8,128)}) %all-gather.13.cloned.1.call-update) | async-done | bytes 1048592 | tf_op jit(solution)/shard_map/all_gather | solution.py:86
  253.3 79.5 %all-gather.11.cloned.1.call-done = f32[8192,128]{1,0:T(8,128)} async-done(((f32[128,128]{1,0:T(8,128)}), f32[8192,128]{1,0:T(8,128)}) %all-gather.11.cloned.1.call-update) | async-done | bytes 4194320 | tf_op jit(solution)/shard_map/all_gather | solution.py:85
  333.0 67.6 %while.62 = (s32[]{:T(128)}, f32[32,128]{1,0:T(8,128)S(1)}, f32[64,32,128]{2,1,0:T(8,128)S(1)}, f32[64,128,128]{2,1,0:T(8,128)}, f32[64,32,128]{2,1,0:T(8,128)}, /*index=5*/s32[]{:T(128)}, s32[]{:T(128)}) while((s32[]{:T(128)}, f32[32,128]{1,0:T(8,128)S(1)}, f32[64,32,128]{2,1,0:T(8,128)S(1)}, f32[64,128,128]{2,1,0:T(8,128)}, ...), condition=%wide.region_5.6_spmd.clone, body=%wide.region_4.5_spmd.clone.sunk | while | flops 6299651 | bytes 164951 | solution.py:65
  402.2 10.6 %all-gather.9.cloned.1.call-done = f32[8192,128]{1,0:T(8,128)} async-done(((f32[128,128]{1,0:T(8,128)}), f32[8192,128]{1,0:T(8,128)}) %all-gather.9.cloned.1.call-update) | async-done | bytes 4194320 | tf_op jit(solution)/shard_map/all_gather | solution.py:94
  412.7 76.9 %all-gather.15.cloned.1.call-done = f32[2048,128]{1,0:T(8,128)} async-done(((f32[32,128]{1,0:T(8,128)}), f32[2048,128]{1,0:T(8,128)}) %all-gather.15.cloned.1.call-update) | async-done | bytes 1048592 | tf_op jit(solution)/shard_map/all_gather | solution.py:95
  489.8 67.6 %while.63 = (s32[]{:T(128)}, f32[32,128]{1,0:T(8,128)S(1)}, f32[64,32,128]{2,1,0:T(8,128)S(1)}, f32[64,128,128]{2,1,0:T(8,128)}, f32[64,32,128]{2,1,0:T(8,128)}, /*index=5*/s32[]{:T(128)}, s32[]{:T(128)}, s32[]{:T(128)}) while((s32[]{:T(128)}, f32[32,128]{1,0:T(8,128)S(1)}, f32[64,32,128]{2,1,0:T(8,128)S(1)}, ...), condition=%wide.region_7.8_spmd.clone, body=%wide.region_6.7_spmd.clone.sunk | while | flops 6299652 | bytes 165482 | solution.py:65
  557.5 46.6 %while.61 = (s32[]{:T(128)}, f32[18,32,128]{2,1,0:T(8,128)S(1)}, f32[16,32,128]{2,1,0:T(8,128)S(1)}, s32[16,4]{1,0:T(8,128)S(1)}, f32[16,4,128,128]{3,2,1,0:T(8,...) while((s32[]{:T(128)}, f32[18,32,128]{2,1,0:T(8,128)S(1)}, ...), condition=%wide.region_9.10_spmd, body=%wide.region_8.9_spmd.sunk | while | flops 31478804 | bytes 595252 | solution.py:55
  (501 shorter events, 227.9 us)
Async XLA Ops:
  7.2 168.6 %copy-start = (f32[1,128,128]{2,1,0:T(8,128)S(1)}, f32[1,128,128]{2,1,0:T(8,128)}, u32[]{:S(2)}) copy-start(f32[1,128,128]{2,1,0:T(8,128)} %param.20) | copy-start | bytes 196612
  7.2 168.6 %copy-start.3 = (f32[1,32,128]{2,1,0:T(8,128)S(1)}, f32[1,32,128]{2,1,0:T(8,128)}, u32[]{:S(2)}) copy-start(f32[1,32,128]{2,1,0:T(8,128)} %param.19) | copy-start | bytes 49156
  7.2 169.5 %copy-start.1 = (f32[1,128,128]{2,1,0:T(8,128)S(1)}, f32[1,128,128]{2,1,0:T(8,128)}, u32[]{:S(2)}) copy-start(f32[1,128,128]{2,1,0:T(8,128)} %param.21) | copy-start | bytes 196612
  7.2 246.1 %all-gather.13.cloned.1.call-start = ((), (), s32[]{:S(2)}) async-start(), calls=%async_computation.2 | async-start | bytes 1064960 | tf_op jit(solution)/shard_map/all_gather | solution.py:86
  166.5 9.3 %collective-permute-start.1 = (f32[32,128]{1,0:T(8,128)S(1)}, f32[32,128]{1,0:T(8,128)S(1)}, u32[]{:S(2)}, u32[]{:S(2)}) collective-permute-start(f32[32,128]{1,0:T(8,128)S(1)} %get-tuple-element.505), channel_id=1, source_target_pairs={{4,0},{8,4},{12,8},{16,12},{20,16},{24,20},{28,24},{32,28},{36,32}... | collective-permute-start | bytes 49160 | tf_op jit(solution)/shard_map/ppermute | solution.py:12
  176.6 156.2 %all-gather.11.cloned.1.call-start = ((), (), s32[]{:S(2)}) async-start(), calls=%async_computation.1 | async-start | bytes 4259840 | tf_op jit(solution)/shard_map/all_gather | solution.py:85
  177.6 235.1 %all-gather.9.cloned.1.call-start = ((), (), s32[]{:S(2)}) async-start(), calls=%async_computation | async-start | bytes 4259840 | tf_op jit(solution)/shard_map/all_gather | solution.py:94
  177.7 5.6 collective-permute-start
  184.1 305.5 %all-gather.15.cloned.1.call-start = ((), (), s32[]{:S(2)}) async-start(), calls=%async_computation.3 | async-start | bytes 1064960 | tf_op jit(solution)/shard_map/all_gather | solution.py:95
  557.4 47.4 %copy-start.2 = (f32[1,32,128]{2,1,0:T(8,128)}, f32[1,32,128]{2,1,0:T(8,128)S(1)}, u32[]{:S(2)}) copy-start(f32[1,32,128]{2,1,0:T(8,128)S(1)} %get-tuple-element.517) | copy-start | bytes 49156
Sparse Core Ops, SparseCore 0:
  176.8 76.5 all-gather.12
  256.1 76.6 all-gather.10
  336.2 76.4 all-gather.8
  415.9 73.6 all-gather.14
where the time goes:
time: 621 us; the launch traced here: 611 us
  waiting for transfers between devices  243 us (39%)
  matrix products  208 us (33%)
  loops' own time  89.2 us (14%)
  local copies, waits for them, and re-layouts  32.9 us (5%)
  blocking collectives  14.4 us (2%)
  between operations  14 us (2%)
  starting transfers between devices  8.42 us (1%)
    dot_general x128, matrix products, walk_advance(): current = jnp.dot(previous, pair[0], precision=HIGH) + pair[1]  131 us
    another operation x1, loops' own time, tree_down(): lax.fori_loop(0, supernodes, tree_advance, (solved, updates))  83.8 us
    all_gather x1, waiting for transfers between devices, shards(): lax.all_gather(map_down[None], 'seg', axis=0, tiled=True)  79.5 us
    all_gather x1, waiting for transfers between devices, shards(): lax.all_gather(offset_up[None], 'seg', axis=0, tiled=True)  76.9 us
    all_gather x1, waiting for transfers between devices, shards(): lax.all_gather(offset_down[None], 'seg', axis=0, tiled=True)  69.2 us
    dot_general x16, matrix products, tree_advance(): jnp.einsum('rc,kac->kra', column, blocks[position], precision=HIGH)  21.6 us
    dot_general x16, matrix products, retreat(): pulled = jnp.einsum('kra,kac->rc', picked, blocks[position], precision=HIGH)  20 us
    dot_general x16, matrix products, tree_advance(): column = jnp.einsum('rb,ab->ra', remain, inverse[position], precision=HIGH)  16.9 us
  transfers between devices with their start and end apart: 6, of which 6 were waited for; matrix products, arithmetic and copies ran while one was open for 11% of the time, Pallas kernels for 0%

commit v1 on v0

v1 whole, which is shorter than its diff:
```python
import jax
import jax.numpy as jnp
from jax import lax
from jax.experimental import pallas as pl
from jax.experimental.pallas import tpu as pltpu
from jax.sharding import PartitionSpec as P

BF = jnp.bfloat16
F32 = jnp.float32
MESH = pl.DeviceIdType.MESH
LOC, KB, R, W = 16, 4, 32, 128
SEGS, SUBS = 64, 4
RING, CHIPS, ROWS = 16, 8, 8


def halves(v):
    high = v.astype(BF)
    return high, (v - high.astype(F32)).astype(BF)


def left_operand(v):
    high, low = halves(v)
    top = jnp.concatenate([high, high], 1)
    bottom = jnp.concatenate([low, jnp.zeros_like(low)], 1)
    return jnp.concatenate([top, bottom], 0)


def folded(left, right, dims):
    both = lax.dot_general(left, right, (dims, ((), ())), preferred_element_type=F32)
    half = both.shape[0] // 2
    return both[:half] + both[half:]


def times(v, w):
    high, low = halves(w)
    return folded(left_operand(v), jnp.concatenate([high, low], 0), ((1,), (0,)))


def times_t(v, w):
    high, low = halves(w)
    return folded(left_operand(v), jnp.concatenate([high, low], 1), ((1,), (1,)))


def t_times(w, v):
    return times(w.T, v)


def chain_kernel(
    pat, rhs_hbm, inv_hbm, off_hbm, sep_rhs_hbm, sep_inv_hbm, coupling_hbm,
    y_ref, own_ref, left_ref,
    rhs, sep_rhs, sep_inv, coupling, small_sem,
    inv, off, acc, vpair, vq, part, xg, rown, rleft, xs, xl, suf_v, suf_q, suf_w, pre_v, pre_z, ends,
    inv_sem, off_sem, pair_ss, pair_rs, z_ss, z_rs, f_ss, f_rs, ring_ss, ring_rs, x_ss, x_rs,
    red_ss, red_rs, lft_ss, lft_rs, fin_ss, fin_rs, nxt_ss, nxt_rs,
):
    s = lax.axis_index("seg")
    u = lax.axis_index("sub")
    core = s % 2
    m = (s // 2) % CHIPS
    i = s % RING
    g = s // RING
    base = s - i

    def send(src, dst, ss, rs, target):
        copy = pltpu.make_async_remote_copy(
            src_ref=src, dst_ref=dst, send_sem=ss, recv_sem=rs, device_id=target, device_id_type=MESH
        )
        copy.start()
        return copy

    def local(hbm, vmem, sem):
        copy = pltpu.make_async_copy(hbm, vmem, sem)
        copy.start()
        return copy

    sibling = (s + 1 - 2 * core, u)
    after = lax.rem(s + 1, SEGS)
    before = lax.rem(s + SEGS - 1, SEGS)

    def ring_peer(k):
        return (base + lax.rem(i + k, RING), u)

    def chip_peer(k):
        return (base + lax.rem(i + 2 * k, RING), u)

    def plane_peer(k):
        return (lax.rem(s + RING * k, SEGS), u)

    def sub_peer(k):
        return (s, lax.rem(u + k, SUBS))

    barrier = pltpu.get_barrier_semaphore()
    greeted = [ring_peer(k) for k in range(1, RING)]
    greeted += [plane_peer(k) for k in range(1, 4)]
    greeted += [sub_peer(k) for k in range(1, SUBS)]
    greeted += [(after, v) for v in range(SUBS)] + [(before, v) for v in range(SUBS)]
    for peer in greeted:
        pl.semaphore_signal(barrier, inc=1, device_id=peer, device_id_type=MESH)

    sep_inv_copy = local(sep_inv_hbm, sep_inv, small_sem.at[0])
    coupling_copy = local(coupling_hbm, coupling, small_sem.at[1])
    rhs_copy = local(rhs_hbm, rhs, small_sem.at[2])
    sep_rhs_copy = local(sep_rhs_hbm, sep_rhs, small_sem.at[3])
    inv_copies = []
    off_copies = []
    for j in range(LOC):
        inv_copies.append(local(inv_hbm.at[j], inv.at[j], inv_sem.at[j]))
        off_copies.append(local(off_hbm.at[j], off.at[j], off_sem.at[j]))

    sep_inv_copy.wait()
    coupling_copy.wait()
    dinv = sep_inv[...]
    own_v = -times(dinv, coupling[...]).T
    own_v = jnp.where(s > 0, own_v, 0.0)
    vpair[core] = own_v

    acc[...] = jnp.zeros_like(acc)
    rhs_copy.wait()

    def down(j):
        inv_copies[j].wait()
        off_copies[j].wait()
        y = times_t(rhs[j] - acc[j].reshape(R, W), inv[j])
        y_ref[j] = y
        products = times_t(y, off[j].reshape(KB * W, W))
        width = LOC + 1 - j
        ids = lax.broadcasted_iota(jnp.int32, (width, 1, ROWS, W), 0) + (j + 1)
        total = acc[j + 1 :]
        for k in range(KB):
            piece = products[:, k * W : (k + 1) * W].reshape(1, SUBS, ROWS, W)
            total = total + jnp.where(ids == pat[k, j], piece, 0.0)
        acc[j + 1 :] = total

    for j in range(0, 8):
        down(j)

    pl.semaphore_wait(barrier, len(greeted))
    pair_copy = send(vpair.at[core], vpair.at[core], pair_ss, pair_rs, sibling)
    for j in range(8, 11):
        down(j)
    pair_copy.wait_recv()
    v0 = vpair[0]
    v1 = vpair[1]
    vm = times(v0, v1)
    vq[m, 0] = vm
    vq[m, 1] = times_t(v0, v0) + times_t(vm, vm)
    z_copies = []
    for k in (4, 3, 5, 2, 6, 1, 7):
        z_copies.append(send(vq.at[m, core], vq.at[m, core], z_ss.at[k - 1], z_rs.at[k - 1], chip_peer(k)))
    for j in range(11, LOC):
        down(j)

    red_copies = []
    for k in range(1, SUBS):
        peer = sub_peer(k)
        red_copies.append(send(acc.at[LOC, peer[1]], rown.at[u], red_ss.at[k - 1], red_rs.at[k - 1], peer))
    for k in range(SUBS):
        v = lax.rem(u + k, SUBS)
        red_copies.append(send(acc.at[LOC + 1, v], rleft.at[u], lft_ss.at[k], lft_rs.at[k], (before, v)))
    rown[u] = acc[LOC, u]
    for copy in red_copies:
        copy.wait_recv()
    sep_rhs_copy.wait()
    left_sum = (rleft[0] + rleft[1]) + (rleft[2] + rleft[3])
    reduced = sep_rhs[u] - ((rown[0] + rown[1]) + (rown[2] + rown[3])) - jnp.where(s < SEGS - 1, left_sum, 0.0)
    phi = times_t(reduced, dinv)
    phi_part = jnp.where(core == 0, times(phi, v1), phi)
    part[i, 0] = phi_part
    part[i, 1] = jnp.where(core == 0, times_t(phi, v0), 0.0) + times_t(phi_part, vm)
    part[i, 2] = phi
    ring_copies = []
    for k in range(1, RING):
        ring_copies.append(send(part.at[i], part.at[i], ring_ss.at[k - 1], ring_rs.at[k - 1], ring_peer(k)))

    f_copies = []
    for copy, k in reversed(list(zip(z_copies, (4, 3, 5, 2, 6, 1, 7)))):
        copy.wait_recv()
        source = lax.rem(m + CHIPS - k, CHIPS)
        f_copies.append(
            send(vq.at[source, core], vq.at[source, core], f_ss.at[k - 1], f_rs.at[k - 1], sibling)
        )
    for copy in ring_copies:
        copy.wait_recv()
    for copy in f_copies:
        copy.wait_recv()

    eye = (
        lax.broadcasted_iota(jnp.int32, (W, W), 0) == lax.broadcasted_iota(jnp.int32, (W, W), 1)
    ).astype(F32)
    suf_v[CHIPS] = eye
    suf_q[CHIPS] = jnp.zeros((W, W), F32)
    suf_w[CHIPS] = jnp.zeros((ROWS, W), F32)
    pre_v[0] = eye
    pre_z[0] = jnp.zeros((ROWS, W), F32)

    def phi_of(n):
        return part[2 * n, 0] + part[2 * n + 1, 0]

    def xi_of(n):
        return part[2 * n, 1] + part[2 * n + 1, 1]

    last = CHIPS - 1
    vs, qs, ps, ws = vq[last, 0], vq[last, 1], phi_of(last), xi_of(last)
    suf_v[last], suf_q[last], suf_w[last] = vs, qs, ws
    pv, pz = vq[0, 0], phi_of(0)
    pre_v[1], pre_z[1] = pv, pz
    for n in reversed(range(last)):
        here = vq[n, 0]
        both = times(jnp.concatenate([here, phi_of(n)], 0), jnp.concatenate([vs, qs], 1))
        vs = both[:W, :W]
        ps = ps + both[W:, :W]
        ahead = jnp.concatenate([both[:W, W:], ws + both[W:, W:]], 0)
        ahead = times_t(ahead, here)
        qs = vq[n, 1] + ahead[:W]
        ws = xi_of(n) + ahead[W:]
        suf_v[n], suf_q[n], suf_w[n] = vs, qs, ws
        up = last - n
        if up < last:
            both = times(jnp.concatenate([pv, pz], 0), vq[up, 0])
            pv, pz = both[:W], both[W:] + phi_of(up)
            pre_v[up + 1], pre_z[up + 1] = pv, pz
    xg[g, :W] = vs
    xg[g, W : 2 * W] = qs
    xg[g, 2 * W : 2 * W + ROWS] = ps
    xg[g, 2 * W + ROWS :] = ws
    x_copies = []
    for k in range(1, 4):
        x_copies.append(send(xg.at[g], xg.at[g], x_ss.at[k - 1], x_rs.at[k - 1], plane_peer(k)))
    for copy in x_copies:
        copy.wait_recv()

    def group(n):
        return xg[n, :W], xg[n, W : 2 * W], xg[n, 2 * W : 2 * W + ROWS], xg[n, 2 * W + ROWS :]

    ga, gb, gc, gd = group(0), group(1), group(2), group(3)
    z1 = ga[2]
    z2 = gb[2] + times(z1, gb[0])
    z3 = gc[2] + times(z2, gc[0])
    w2 = gd[3] + times(z3, gd[1])
    w1 = gc[3] + times(z2, gc[1]) + times_t(w2, gc[0])
    w0 = gb[3] + times(z1, gb[1]) + times_t(w1, gb[0])
    none = jnp.zeros((ROWS, W), F32)
    ends[0, 0], ends[0, 1] = none, w0
    ends[1, 0], ends[1, 1] = z1, w1
    ends[2, 0], ends[2, 1] = z2, w2
    ends[3, 0], ends[3, 1] = z3, none
    z_in = ends[g, 0]
    w_in = ends[g, 1]
    z_chip = pre_z[m] + times(z_in, pre_v[m])
    z_next = part[2 * m, 0] + part[2 * m + 1, 0] + times(z_chip, vm)
    w_chip = suf_w[m + 1] + times(z_next, suf_q[m + 1]) + times_t(w_in, suf_v[m + 1])
    z_even = part[2 * m, 2] + times(z_chip, v0)
    z_odd = part[2 * m + 1, 2] + times(z_even, v1)
    w_even = times_t(z_odd + w_chip, v1)
    x = times(jnp.where(core == 0, z_even + w_even, z_odd + w_chip), dinv)
    xs[u] = x
    fin_copies = []
    for k in range(1, SUBS):
        fin_copies.append(send(xs.at[u], xs.at[u], fin_ss.at[k - 1], fin_rs.at[k - 1], sub_peer(k)))
    for k in range(SUBS):
        v = lax.rem(u + k, SUBS)
        fin_copies.append(send(xs.at[u], xl.at[u], nxt_ss.at[k], nxt_rs.at[k], (after, v)))
    for copy in fin_copies:
        copy.wait_recv()
    own_ref[...] = xs[...].reshape(R, W)
    left_ref[...] = jnp.where(s > 0, xl[...].reshape(R, W), 0.0)

    for copy in [pair_copy] + z_copies + red_copies + ring_copies + f_copies + x_copies + fin_copies:
        copy.wait_send()


def up_kernel(pat, y, own, left, inv_hbm, off_hbm, x_ref, inv, off, known, inv_sem, off_sem):
    inv_copies = {}
    off_copies = {}
    for j in reversed(range(LOC)):
        inv_copies[j] = pltpu.make_async_copy(inv_hbm.at[j], inv.at[j], inv_sem.at[j])
        off_copies[j] = pltpu.make_async_copy(off_hbm.at[j], off.at[j], off_sem.at[j])
        inv_copies[j].start()
        off_copies[j].start()
    known[:LOC] = jnp.zeros_like(y)
    known[LOC] = own[...]
    known[LOC + 1] = left[...]
    for j in reversed(range(LOC)):
        inv_copies[j].wait()
        off_copies[j].wait()
        pulled = y[j]
        for k in range(KB):
            target = pat[k, j]
            weight = jnp.where(target >= 0, 1.0, 0.0).astype(F32)
            pulled = pulled - times(known[jnp.maximum(target, 0)] * weight, off[j, k])
        x = times(pulled, inv[j])
        known[j] = x
        x_ref[j] = x


IN_VMEM = pl.BlockSpec(memory_space=pltpu.VMEM)
IN_SMEM = pl.BlockSpec(memory_space=pltpu.SMEM)
IN_HBM = pl.BlockSpec(memory_space=pltpu.HBM)


def rows_of(*shape):
    return jax.ShapeDtypeStruct(shape, F32)


def shards(rhs_local, diag_inv, off_blocks, pattern, sep_rhs, sep_inv, coupling):
    rhs = rhs_local[0, 0]
    inverse = diag_inv[0, 0]
    blocks = off_blocks[0, 0]
    targets = pattern[0, 0].T
    dma = pltpu.SemaphoreType.DMA
    vmem = pltpu.VMEM
    solved, own, left = pl.pallas_call(
        chain_kernel,
        name="down_and_chain",
        out_shape=(rows_of(LOC, R, W), rows_of(R, W), rows_of(R, W)),
        in_specs=[IN_SMEM] + [IN_HBM] * 6,
        out_specs=(IN_VMEM, IN_VMEM, IN_VMEM),
        scratch_shapes=[
            vmem((LOC, R, W), F32),
            vmem((SUBS, ROWS, W), F32),
            vmem((W, W), F32),
            vmem((W, W), F32),
            dma((4,)),
            vmem((LOC, W, W), F32),
            vmem((LOC, KB, W, W), F32),
            vmem((LOC + 2, SUBS, ROWS, W), F32),
            vmem((2, W, W), F32),
            vmem((CHIPS, 2, W, W), F32),
            vmem((RING, 3, ROWS, W), F32),
            vmem((4, 2 * W + 2 * ROWS, W), F32),
            vmem((SUBS, ROWS, W), F32),
            vmem((SUBS, ROWS, W), F32),
            vmem((SUBS, ROWS, W), F32),
            vmem((SUBS, ROWS, W), F32),
            vmem((CHIPS + 1, W, W), F32),
            vmem((CHIPS + 1, W, W), F32),
            vmem((CHIPS + 1, ROWS, W), F32),
            vmem((CHIPS, W, W), F32),
            vmem((CHIPS, ROWS, W), F32),
            vmem((4, 2, ROWS, W), F32),
            dma((LOC,)), dma((LOC,)),
            dma(()), dma(()),
            dma((7,)), dma((7,)),
            dma((7,)), dma((7,)),
            dma((15,)), dma((15,)),
            dma((3,)), dma((3,)),
            dma((3,)), dma((3,)),
            dma((4,)), dma((4,)),
            dma((3,)), dma((3,)),
            dma((4,)), dma((4,)),
        ],
        compiler_params=pltpu.CompilerParams(
            collective_id=0, has_side_effects=True, vmem_limit_bytes=62 << 20
        ),
    )(targets, rhs, inverse, blocks, sep_rhs[0].reshape(SUBS, ROWS, W), sep_inv[0], coupling[0])
    tree_solution = pl.pallas_call(
        up_kernel,
        name="up",
        out_shape=rows_of(LOC, R, W),
        in_specs=[IN_SMEM, IN_VMEM, IN_VMEM, IN_VMEM, IN_HBM, IN_HBM],
        out_specs=IN_VMEM,
        scratch_shapes=[
            vmem((LOC, W, W), F32),
            vmem((LOC, KB, W, W), F32),
            vmem((LOC + 2, R, W), F32),
            dma((LOC,)),
            dma((LOC,)),
        ],
        compiler_params=pltpu.CompilerParams(vmem_limit_bytes=62 << 20),
    )(targets, solved, own, left, inverse, blocks)
    return tree_solution[None, None], own[None]


def solution(mesh):
    in_specs = (
        P("seg", "sub", None, None, None),
        P("seg", "sub", None, None, None),
        P("seg", "sub", None, None, None, None),
        P("seg", "sub", None, None),
        P("seg", None, None),
        P("seg", None, None),
        P("seg", None, None),
    )
    out_specs = (P("seg", "sub", None, None, None), P("seg", None, None))
    return jax.shard_map(shards, mesh=mesh, in_specs=in_specs, out_specs=out_specs, check_vma=False)
```

time: 621 us -> 65 us (0.10); the launches traced: 611 us -> 64.9 us
  waiting for transfers between devices: 243 us -> 0 us
  matrix products: 208 us -> 0 us
  loops' own time: 89.2 us -> 0 us
  Pallas kernels: 0 us -> 63.6 us
  local copies, waits for them, and re-layouts: 32.9 us -> 0.61 us
  blocking collectives: 14.4 us -> 0 us
  between operations: 14 us -> 0.66 us
  starting transfers between devices: 8.42 us -> 0 us
    all_gather x4 -> x0, waiting for transfers between devices: 236 us -> none  [the longest x1 79.5 us: shards(): lax.all_gather(map_down[None], 'seg', axis=0, tiled=True)]
    dot_general x196 -> x0, matrix products: 208 us -> none  [the longest x128 131 us: walk_advance(): current = jnp.dot(previous, pair[0], precision=HIGH) + pair[1]]
    another operation x4 -> x0, loops' own time: 89.2 us -> none  [the longest x1 83.8 us: tree_down(): lax.fori_loop(0, supernodes, tree_advance, (solved, updates))]
    pallas_call x0 -> x2, Pallas kernels: none -> 63.6 us  [the longest x1 55.7 us: shards(): pl.pallas_call(chain_kernel, name='down_and_chain', out_shape=(rows_of(LO...]
    psum x1 -> x0, blocking collectives: 14.4 us -> none  [shards(): own_total, left_total = lax.psum((own_term, left_term), 'sub')]
    dynamic_slice x16 -> x0, local copies, waits for them, and re-layouts: 12.1 us -> none  [tree_advance(): row_targets = targets[position]]
    slice x16 -> x0, local copies, waits for them, and re-layouts: 9.73 us -> none  [tree_advance(): target = jnp.maximum(row_targets[slot_number], 0)]
    gather x16 -> x0, local copies, waits for them, and re-layouts: 8.84 us -> none  [retreat(): picked = known_rows[jnp.maximum(row_targets, 0)] * weight_on]
  transfers between devices with their start and end apart: 6 -> 0, of which waited for: 6 -> 0; matrix products, arithmetic and copies ran while one was open for 11% -> 0% of each run, Pallas kernels for 0% -> 0%
where the time goes in v1:
time: 65 us; the launch traced here: 64.9 us
  Pallas kernels  63.6 us (98%)
  between operations  0.66 us (1%)
    pallas_call x1, Pallas kernels, shards(): pl.pallas_call(chain_kernel, name='down_and_chain', out_shape=(rows_of(LO...  55.7 us
    pallas_call x1, Pallas kernels, shards(): pl.pallas_call(up_kernel, name='up', out_shape=rows_of(LOC, R, W), in_spe...  7.94 us

profile of v1, /device:TPU:1, one launch (start us, length us, event | category | flops | bytes accessed | tf_op | source)
XLA Modules:
  0.0 64.9 jit_solution(14895167679062703800)
XLA Ops:
  0.6 55.7 %down_and_chain.1 = (f32[16,32,128]{2,1,0:T(8,128)}, f32[32,128]{1,0:T(8,128)}, f32[32,128]{1,0:T(8,128)}) custom-call(s32[4,16]{1,0:T(4,128)} %bitcast.21, f32[16,32,128]{2,1,0:T(8,128)} %bitcast.15, f32[16,128,128]{2,1,0:T(8,128)} %bitcast.13, f32[16,4,128,128]{3,2,1,0:T(8,128)} %bitcast.11, f32[4,8,128]{2,1,0:T(8,128)} %bitcast.20, f32[128,128]{1,0:T(8,128)} %bitcast.17, ...), custom_call_target="tpu_custom_call" | custom-call | tf_op jit(solution)/shard_map/down_and_chain/pallas_call | solution.py:312
  56.3 0.0 copy-start
  56.3 7.9 %up.1 = f32[16,32,128]{2,1,0:T(8,128)} custom-call(s32[4,16]{1,0:T(4,128)} %bitcast.22, f32[16,32,128]{2,1,0:T(8,128)} %get-tuple-element.5.y, f32[32,128]{1,0:T(8,128)} %get-tuple-element.6.own, f32[32,128]{1,0:T(8,128)} %get-tuple-element.7.left, f32[16,128,128]{2,1,0:T(8,128)} %bitcast.14, f32[16,4,128,128]{3,2,1,0:T(8,128)} %bitcast.12), custom_call_target="tpu_custom_call" | custom-call | tf_op jit(solution)/shard_map/up/pallas_call | solution.py:356
  64.3 0.0 copy-done
  64.3 0.6 copy.10
Async XLA Ops:
  56.3 8.0 %copy-start = (f32[32,128]{1,0:T(8,128)S(1)}, f32[32,128]{1,0:T(8,128)}, u32[]{:S(2)}) copy-start(f32[32,128]{1,0:T(8,128)} %get-tuple-element.6.own) | copy-start | bytes 49156

commit v2 on v1

v2 whole, which is shorter than its diff:
```python
import jax
import jax.numpy as jnp
from jax import lax
from jax.experimental import pallas as pl
from jax.experimental.pallas import tpu as pltpu
from jax.sharding import PartitionSpec as P

BF = jnp.bfloat16
F32 = jnp.float32
MESH = pl.DeviceIdType.MESH
LOC, KB, R, W = 16, 4, 32, 128
SEGS, SUBS = 64, 4
RING, CHIPS, ROWS = 16, 8, 8


def halves(v):
    high = v.astype(BF)
    return high, (v - high.astype(F32)).astype(BF)


def left_operand(v):
    high, low = halves(v)
    top = jnp.concatenate([high, high], 1)
    bottom = jnp.concatenate([low, jnp.zeros_like(low)], 1)
    return jnp.concatenate([top, bottom], 0)


def folded(left, right, dims):
    both = lax.dot_general(left, right, (dims, ((), ())), preferred_element_type=F32)
    half = both.shape[0] // 2
    return both[:half] + both[half:]


def times(v, w):
    high, low = halves(w)
    return folded(left_operand(v), jnp.concatenate([high, low], 0), ((1,), (0,)))


def times_t(v, w):
    high, low = halves(w)
    return folded(left_operand(v), jnp.concatenate([high, low], 1), ((1,), (1,)))


def t_times(w, v):
    return times(w.T, v)


def solve_kernel(
    pat, rhs_hbm, inv_hbm, off_hbm, sep_rhs_hbm, sep_inv_hbm, coupling_hbm,
    x_ref, own_ref,
    rhs, sep_rhs, sep_inv, coupling, small_sem,
    inv, off, acc, ys, prev_inv, vpair, vq, part, mine, xg, xr, terms, xs,
    suf_v, suf_q, suf_w, pre_v, pre_z, ends, g_high, g_low, given, known_high, known_low,
    inv_sem, off_sem, prev_ss, prev_rs, pair_ss, pair_rs, z_ss, z_rs, f_ss, f_rs, ring_ss, ring_rs,
    mine_ss, mine_rs, x_ss, x_rs, h_ss, h_rs, r_ss, r_rs, red_ss, red_rs, fin_ss, fin_rs,
):
    s = lax.axis_index("seg")
    u = lax.axis_index("sub")
    core = s % 2
    m = (s // 2) % CHIPS
    i = s % RING
    g = s // RING
    base = s - i
    first_core = core == 0

    def send(src, dst, ss, rs, target):
        copy = pltpu.make_async_remote_copy(
            src_ref=src, dst_ref=dst, send_sem=ss, recv_sem=rs, device_id=target, device_id_type=MESH
        )
        copy.start()
        return copy

    def local(hbm, vmem, sem):
        copy = pltpu.make_async_copy(hbm, vmem, sem)
        copy.start()
        return copy

    sibling = (s + 1 - 2 * core, u)
    after = (lax.rem(s + 1, SEGS), u)
    before = (lax.rem(s + SEGS - 1, SEGS), u)

    def ring_peer(k):
        return (base + lax.rem(i + k, RING), u)

    def chip_peer(k):
        return (base + lax.rem(i + 2 * k, RING), u)

    def plane_peer(k):
        return (lax.rem(s + RING * k, SEGS), u)

    def sub_peer(k):
        return (s, lax.rem(u + k, SUBS))

    barrier = pltpu.get_barrier_semaphore()
    greeted = [ring_peer(k) for k in (8, 7, 9, 6, 10, 5, 11, 4, 12, 3, 13, 2, 14, 1, 15)]
    greeted += [plane_peer(k) for k in (2, 1, 3)]
    greeted += [sub_peer(k) for k in (2, 1, 3)]
    greeted += [after, before]
    for peer in greeted:
        pl.semaphore_signal(barrier, inc=1, device_id=peer, device_id_type=MESH)

    sep_inv_copy = local(sep_inv_hbm, sep_inv, small_sem.at[0])
    coupling_copy = local(coupling_hbm, coupling, small_sem.at[1])
    rhs_copy = local(rhs_hbm, rhs, small_sem.at[2])
    sep_rhs_copy = local(sep_rhs_hbm, sep_rhs, small_sem.at[3])
    inv_copies = []
    off_copies = []
    for j in range(LOC):
        inv_copies.append(local(inv_hbm.at[j], inv.at[j], inv_sem.at[j]))
        off_copies.append(local(off_hbm.at[j], off.at[j], off_sem.at[j]))

    sep_inv_copy.wait()
    coupling_copy.wait()
    dinv = sep_inv[...]
    own_v = -times(dinv, coupling[...]).T
    own_v = jnp.where(s > 0, own_v, 0.0)
    vpair[core] = own_v

    acc[...] = jnp.zeros_like(acc)
    rhs_copy.wait()

    def down(j):
        inv_copies[j].wait()
        off_copies[j].wait()
        y = times_t(rhs[j] - acc[j].reshape(R, W), inv[j])
        ys[j] = y
        products = times_t(y, off[j].reshape(KB * W, W))
        width = LOC + 1 - j
        ids = lax.broadcasted_iota(jnp.int32, (width, 1, ROWS, W), 0) + (j + 1)
        total = acc[j + 1 :]
        for k in range(KB):
            piece = products[:, k * W : (k + 1) * W].reshape(1, SUBS, ROWS, W)
            total = total + jnp.where(ids == pat[k, j], piece, 0.0)
        acc[j + 1 :] = total

    def prepare_up(j):
        stacked = jnp.concatenate([off[j].reshape(KB * W, W), ys[j]], 0)
        both = times(stacked, inv[j])
        high, low = halves(both[: KB * W])
        g_high[j] = high
        g_low[j] = low
        given[j] = both[KB * W :]

    for j in range(0, 8):
        down(j)

    pl.semaphore_wait(barrier, len(greeted))
    pair_copy = send(vpair.at[core], vpair.at[core], pair_ss, pair_rs, sibling)
    prev_copy = send(sep_inv, prev_inv, prev_ss, prev_rs, after)
    for j in range(8, 10):
        down(j)
    pair_copy.wait_recv()
    v0 = vpair[0]
    v1 = vpair[1]
    vm = times(v0, v1)
    vq[m, 0] = vm
    vq[m, 1] = times_t(v0, v0) + times_t(vm, vm)
    z_copies = {}
    f_copies = []

    def z_send(way, step, piece):
        source = lax.rem(m + (CHIPS + 1 - step if way == 0 else step - 1), CHIPS)
        where = vq.at[source, core, pl.ds(piece * (W // 2), W // 2)]
        index = way * 8 + (step - 1) * 2 + piece
        z_copies[way, step, piece] = send(
            where, where, z_ss.at[index], z_rs.at[index], chip_peer(1 if way == 0 else CHIPS - 1)
        )

    def f_send(distance, index):
        where = vq.at[lax.rem(m + CHIPS + distance, CHIPS), core]
        f_copies.append(send(where, where, f_ss.at[index], f_rs.at[index], sibling))

    def z_step(step):
        for piece in range(2):
            for way in range(2):
                z_copies[way, step - 1, piece].wait_recv()
                if step < 4 or way == piece:
                    z_send(way, step, piece)
        f_send(1 - step, step - 2)
        f_send(step - 1, step + 1)

    for piece in range(2):
        for way in range(2):
            z_send(way, 1, piece)
    for j in range(10, LOC):
        down(j)

    red_copies = []
    for k in (2, 1, 3):
        peer = sub_peer(k)
        red_copies.append(
            send(acc.at[pl.ds(LOC, 2), peer[1]], terms.at[u], red_ss.at[k - 1], red_rs.at[k - 1], peer)
        )
    terms[u] = acc[LOC:, u]
    z_step(2)
    for j in range(4):
        prepare_up(j)
    z_step(3)
    for j in range(4, 6):
        prepare_up(j)
    sep_rhs_copy.wait()
    for copy in red_copies:
        copy.wait_recv()
    prev_copy.wait_recv()
    summed = (terms[0] + terms[1]) + (terms[2] + terms[3])
    delta = jnp.where(s > 0, -times_t(summed[1], prev_inv[...]), 0.0)
    phi = times_t(sep_rhs[u] - summed[0], dinv) + times(delta, vpair[core])
    phi_part = jnp.where(first_core, times(phi, v1), phi)
    part[i, 0] = phi_part
    part[i, 1] = (
        times_t(jnp.where(first_core, phi, delta), v0)
        + jnp.where(first_core, delta, 0.0)
        + times_t(phi_part, vm)
    )
    mine[core, 0] = phi
    mine[core, 1] = delta
    ring_copies = []
    for k in (8, 7, 9, 6, 10, 5, 11, 4, 12, 3, 13, 2, 14, 1, 15):
        ring_copies.append(send(part.at[i], part.at[i], ring_ss.at[k - 1], ring_rs.at[k - 1], ring_peer(k)))
    mine_copy = send(mine.at[core], mine.at[core], mine_ss, mine_rs, sibling)

    z_step(4)
    for j in range(6, 9):
        prepare_up(j)
    z_copies[0, 4, 0].wait_recv()
    z_copies[1, 4, 1].wait_recv()
    f_send(4, 6)
    for copy in f_copies:
        copy.wait_recv()

    eye = (
        lax.broadcasted_iota(jnp.int32, (W, W), 0) == lax.broadcasted_iota(jnp.int32, (W, W), 1)
    ).astype(F32)
    suf_v[CHIPS] = eye
    suf_q[CHIPS] = jnp.zeros((W, W), F32)
    suf_w[CHIPS] = jnp.zeros((ROWS, W), F32)
    pre_v[0] = eye
    pre_z[0] = jnp.zeros((ROWS, W), F32)
    last = CHIPS - 1
    vs, qs = vq[last, 0], vq[last, 1]
    suf_v[last], suf_q[last] = vs, qs
    pv = vq[0, 0]
    pre_v[1] = pv
    for n in reversed(range(last)):
        both = times(vq[n, 0], jnp.concatenate([vs, qs], 1))
        vs = both[:, :W]
        qs = vq[n, 1] + times_t(both[:, W:], vq[n, 0])
        suf_v[n], suf_q[n] = vs, qs
        up = last - n
        if up < last:
            pv = times(pv, vq[up, 0])
            pre_v[up + 1] = pv
    xg[g, 0] = vs
    xg[g, 1] = qs
    x_copies = []
    for k in (2, 1, 3):
        x_copies.append(send(xg.at[g, core], xg.at[g, core], x_ss.at[k - 1], x_rs.at[k - 1], plane_peer(k)))

    mine_copy.wait_recv()
    for copy in ring_copies:
        copy.wait_recv()

    phis = [part[2 * n, 0] + part[2 * n + 1, 0] for n in range(CHIPS)]
    xis = [part[2 * n, 1] + part[2 * n + 1, 1] for n in range(CHIPS)]
    ps, ws, pz = phis[last], xis[last], phis[0]
    suf_w[last] = ws
    pre_z[1] = pz
    for n in reversed(range(last)):
        ps = ps + times(phis[n], suf_v[n + 1])
        ws = xis[n] + times_t(ws + times(phis[n], suf_q[n + 1]), vq[n, 0])
        suf_w[n] = ws
        up = last - n
        if up < last:
            pz = phis[up] + times(pz, vq[up, 0])
            pre_z[up + 1] = pz
    xr[g, 0] = ps
    xr[g, 1] = ws
    r_copies = []
    for k in (2, 1, 3):
        r_copies.append(send(xr.at[g], xr.at[g], r_ss.at[k - 1], r_rs.at[k - 1], plane_peer(k)))
    known_high[...] = jnp.zeros_like(known_high)
    known_low[...] = jnp.zeros_like(known_low)
    h_copies = []
    for k in (1, 3, 2):
        x_copies[(2, 1, 3).index(k)].wait_recv()
        source = lax.rem(g + 4 - k, 4)
        h_copies.append(
            send(xg.at[source, core], xg.at[source, core], h_ss.at[k - 1], h_rs.at[k - 1], sibling)
        )
    for j in range(9, LOC):
        prepare_up(j)
    for copy in h_copies + r_copies:
        copy.wait_recv()

    def group(n):
        return xg[n, 0], xg[n, 1], xr[n, 0], xr[n, 1]

    ga, gb, gc, gd = group(0), group(1), group(2), group(3)
    z1 = ga[2]
    z2 = gb[2] + times(z1, gb[0])
    z3 = gc[2] + times(z2, gc[0])
    w2 = gd[3] + times(z3, gd[1])
    w1 = gc[3] + times(z2, gc[1]) + times_t(w2, gc[0])
    w0 = gb[3] + times(z1, gb[1]) + times_t(w1, gb[0])
    none = jnp.zeros((ROWS, W), F32)
    ends[0, 0], ends[0, 1] = none, w0
    ends[1, 0], ends[1, 1] = z1, w1
    ends[2, 0], ends[2, 1] = z2, w2
    ends[3, 0], ends[3, 1] = z3, none
    z_in = ends[g, 0]
    w_in = ends[g, 1]
    z_chip = pre_z[m] + times(z_in, pre_v[m])
    z_next = part[2 * m, 0] + part[2 * m + 1, 0] + times(z_chip, vm)
    w_chip = suf_w[m + 1] + times(z_next, suf_q[m + 1]) + times_t(w_in, suf_v[m + 1])
    z_even = mine[0, 0] + times(z_chip, v0)
    odd = mine[1, 0] + times(z_even, v1) + w_chip
    even = z_even + times_t(odd, v1) + mine[1, 1]
    outer = z_chip + times_t(even, v0) + mine[0, 1]
    xs[u, 0] = times(jnp.where(first_core, even, odd), dinv)
    xs[u, 1] = jnp.where(s > 0, times(jnp.where(first_core, outer, even), prev_inv[...]), 0.0)
    fin_copies = []
    for k in (2, 1, 3):
        fin_copies.append(send(xs.at[u], xs.at[u], fin_ss.at[k - 1], fin_rs.at[k - 1], sub_peer(k)))
    for copy in fin_copies:
        copy.wait_recv()

    def learn(t, x):
        high, low = halves(x)
        known_high[t] = high
        known_low[t] = low

    own = jnp.concatenate([xs[v, 0] for v in range(SUBS)], 0)
    own_ref[...] = own
    learn(LOC, own)
    learn(LOC + 1, jnp.concatenate([xs[v, 1] for v in range(SUBS)], 0))
    for j in reversed(range(LOC)):
        places = []
        for k in range(KB):
            target = pat[k, j]
            places.append(jnp.where(target >= 0, target, LOC + 2))
        high = jnp.concatenate([known_high[t] for t in places], 1)
        low = jnp.concatenate([known_low[t] for t in places], 1)
        pulled = folded(jnp.concatenate([high, low], 0), g_high[j], ((1,), (0,)))
        pulled += jnp.dot(high, g_low[j], preferred_element_type=F32)
        x = given[j] - pulled
        learn(j, x)
        x_ref[j] = x

    started = [pair_copy, prev_copy, mine_copy] + list(z_copies.values()) + red_copies + ring_copies + r_copies
    for copy in started + f_copies + x_copies + h_copies + fin_copies:
        copy.wait_send()


def store_kernel(x, own, x_out, own_out, x_sem, own_sem):
    x_copy = pltpu.make_async_copy(x, x_out, x_sem)
    own_copy = pltpu.make_async_copy(own, own_out, own_sem)
    x_copy.start()
    own_copy.start()
    x_copy.wait()
    own_copy.wait()


IN_VMEM = pl.BlockSpec(memory_space=pltpu.VMEM)
IN_SMEM = pl.BlockSpec(memory_space=pltpu.SMEM)
IN_HBM = pl.BlockSpec(memory_space=pltpu.HBM)


def rows_of(*shape):
    return jax.ShapeDtypeStruct(shape, F32)


def shards(rhs_local, diag_inv, off_blocks, pattern, sep_rhs, sep_inv, coupling):
    rhs = rhs_local[0, 0]
    inverse = diag_inv[0, 0]
    blocks = off_blocks[0, 0]
    targets = pattern[0, 0].T
    dma = pltpu.SemaphoreType.DMA
    vmem = pltpu.VMEM
    tree_solution, own = pl.pallas_call(
        solve_kernel,
        name="solve",
        out_shape=(rows_of(LOC, R, W), rows_of(R, W)),
        in_specs=[IN_SMEM] + [IN_HBM] * 6,
        out_specs=(IN_VMEM, IN_VMEM),
        scratch_shapes=[
            vmem((LOC, R, W), F32),
            vmem((SUBS, ROWS, W), F32),
            vmem((W, W), F32),
            vmem((W, W), F32),
            dma((4,)),
            vmem((LOC, W, W), F32),
            vmem((LOC, KB, W, W), F32),
            vmem((LOC + 2, SUBS, ROWS, W), F32),
            vmem((LOC, R, W), F32),
            vmem((W, W), F32),
            vmem((2, W, W), F32),
            vmem((CHIPS, 2, W, W), F32),
            vmem((RING, 2, ROWS, W), F32),
            vmem((2, 2, ROWS, W), F32),
            vmem((4, 2, W, W), F32),
            vmem((4, 2, ROWS, W), F32),
            vmem((SUBS, 2, ROWS, W), F32),
            vmem((SUBS, 2, ROWS, W), F32),
            vmem((CHIPS + 1, W, W), F32),
            vmem((CHIPS + 1, W, W), F32),
            vmem((CHIPS + 1, ROWS, W), F32),
            vmem((CHIPS, W, W), F32),
            vmem((CHIPS, ROWS, W), F32),
            vmem((4, 2, ROWS, W), F32),
            vmem((LOC, KB * W, W), BF),
            vmem((LOC, KB * W, W), BF),
            vmem((LOC, R, W), F32),
            vmem((LOC + 3, R, W), BF),
            vmem((LOC + 3, R, W), BF),
            dma((LOC,)), dma((LOC,)),
            dma(()), dma(()),
            dma(()), dma(()),
            dma((16,)), dma((16,)),
            dma((7,)), dma((7,)),
            dma((15,)), dma((15,)),
            dma(()), dma(()),
            dma((3,)), dma((3,)),
            dma((3,)), dma((3,)),
            dma((3,)), dma((3,)),
            dma((3,)), dma((3,)),
            dma((3,)), dma((3,)),
        ],
        compiler_params=pltpu.CompilerParams(
            collective_id=0, has_side_effects=True, vmem_limit_bytes=62 << 20
        ),
    )(targets, rhs, inverse, blocks, sep_rhs[0].reshape(SUBS, ROWS, W), sep_inv[0], coupling[0])
    tree_solution, own = pl.pallas_call(
        store_kernel,
        name="store",
        out_shape=(rows_of(LOC, R, W), rows_of(R, W)),
        in_specs=[IN_VMEM, IN_VMEM],
        out_specs=(IN_HBM, IN_HBM),
        scratch_shapes=[dma(()), dma(())],
    )(tree_solution, own)
    return tree_solution[None, None], own[None]


def solution(mesh):
    in_specs = (
        P("seg", "sub", None, None, None),
        P("seg", "sub", None, None, None),
        P("seg", "sub", None, None, None, None),
        P("seg", "sub", None, None),
        P("seg", None, None),
        P("seg", None, None),
        P("seg", None, None),
    )
    out_specs = (P("seg", "sub", None, None, None), P("seg", None, None))
    return jax.shard_map(shards, mesh=mesh, in_specs=in_specs, out_specs=out_specs, check_vma=False)
```

time: 65 us -> 51.8 us (0.80)
  Pallas kernels: 63.6 us -> 51.1 us
    pallas_call x2, Pallas kernels: 63.6 us -> 51.1 us  [the longest x1 49.4 us: shards(): pl.pallas_call(solve_kernel, name='solve', out_shape=(rows_of(LOC, R, W),...]
where the time goes in v2:
time: 51.8 us; the launch traced here: 51.7 us
  Pallas kernels  51.1 us (99%)
  between operations  0.64 us (1%)
    pallas_call x1, Pallas kernels, shards(): pl.pallas_call(solve_kernel, name='solve', out_shape=(rows_of(LOC, R, W),...  49.4 us
    pallas_call x1, Pallas kernels, shards(): pl.pallas_call(store_kernel, name='store', out_shape=(rows_of(LOC, R, W),...  1.67 us

profile of v2, /device:TPU:1, one launch (start us, length us, event | category | flops | bytes accessed | tf_op | source)
XLA Modules:
  0.0 51.7 jit_solution(17582049747799868842)
XLA Ops:
  0.6 49.4 %solve.1 = (f32[16,32,128]{2,1,0:T(8,128)}, f32[32,128]{1,0:T(8,128)}) custom-call(s32[4,16]{1,0:T(4,128)} %bitcast.17, f32[16,32,128]{2,1,0:T(8,128)} %bitcast.13, f32[16,128,128]{2,1,0:T(8,128)} %bitcast.12, f32[16,4,128,128]{3,2,1,0:T(8,128)} %bitcast.11, f32[4,8,128]{2,1,0:T(8,128)} %bitcast.16, f32[128,128]{1,0:T(8,128)} %bitcast.14, f32[128,128]{1,0:T(8,128)} %bitcast.15), custom_call_target="tpu_custom_call" | custom-call | tf_op jit(solution)/shard_map/solve/pallas_call | solution.py:379
  50.0 1.7 %store.1 = (f32[16,32,128]{2,1,0:T(8,128)}, f32[32,128]{1,0:T(8,128)}) custom-call(f32[16,32,128]{2,1,0:T(8,128)} %get-tuple-element.6.x, f32[32,128]{1,0:T(8,128)} %get-tuple-element.7.own), custom_call_target="tpu_custom_call" | custom-call | tf_op jit(solution)/shard_map/store/pallas_call | solution.py:432

commit v3 on v2

--- a/solution.py
+++ b/solution.py
@@ -49,9 +49,9 @@
     pat, rhs_hbm, inv_hbm, off_hbm, sep_rhs_hbm, sep_inv_hbm, coupling_hbm,
     x_ref, own_ref,
     rhs, sep_rhs, sep_inv, coupling, small_sem,
-    inv, off, acc, ys, prev_inv, vpair, vq, part, mine, xg, xr, terms, xs,
+    inv, off, acc, ys, prev_inv, vr, vq, part, mine, xg, xr, terms, xs,
     suf_v, suf_q, suf_w, pre_v, pre_z, ends, g_high, g_low, given, known_high, known_low,
-    inv_sem, off_sem, prev_ss, prev_rs, pair_ss, pair_rs, z_ss, z_rs, f_ss, f_rs, ring_ss, ring_rs,
+    inv_sem, off_sem, prev_ss, prev_rs, relays, z_ss, z_rs, f_ss, f_rs, ring_ss, ring_rs,
     mine_ss, mine_rs, x_ss, x_rs, h_ss, h_rs, r_ss, r_rs, red_ss, red_rs, fin_ss, fin_rs,
 ):
     s = lax.axis_index("seg")
@@ -79,9 +79,6 @@
     after = (lax.rem(s + 1, SEGS), u)
     before = (lax.rem(s + SEGS - 1, SEGS), u)
 
-    def ring_peer(k):
-        return (base + lax.rem(i + k, RING), u)
-
     def chip_peer(k):
         return (base + lax.rem(i + 2 * k, RING), u)
 
@@ -92,36 +89,32 @@
         return (s, lax.rem(u + k, SUBS))
 
     barrier = pltpu.get_barrier_semaphore()
-    greeted = [ring_peer(k) for k in (8, 7, 9, 6, 10, 5, 11, 4, 12, 3, 13, 2, 14, 1, 15)]
-    greeted += [plane_peer(k) for k in (2, 1, 3)]
-    greeted += [sub_peer(k) for k in (2, 1, 3)]
-    greeted += [after, before]
+    far_first = (4, 3, 5, 2, 6, 1, 7)
+    chip_sides = (chip_peer(1), chip_peer(CHIPS - 1))
+    greeted = [after, before, sibling, *chip_sides]
+    greeted += [plane_peer(1), plane_peer(3), sub_peer(1), sub_peer(3)]
     for peer in greeted:
         pl.semaphore_signal(barrier, inc=1, device_id=peer, device_id_type=MESH)
 
-    sep_inv_copy = local(sep_inv_hbm, sep_inv, small_sem.at[0])
-    coupling_copy = local(coupling_hbm, coupling, small_sem.at[1])
     rhs_copy = local(rhs_hbm, rhs, small_sem.at[2])
+    tree_copies = {}
+    for n, (low, high) in enumerate(((0, 1), (1, 2), (2, 4), (4, 8), (8, 16))):
+        run = pl.ds(low, high - low)
+        tree_copies[low] = (
+            local(inv_hbm.at[run], inv.at[run], inv_sem.at[n]),
+            local(off_hbm.at[run], off.at[run], off_sem.at[n]),
+        )
+        if n == 1:
+            sep_inv_copy = local(sep_inv_hbm, sep_inv, small_sem.at[0])
+            coupling_copy = local(coupling_hbm, coupling, small_sem.at[1])
     sep_rhs_copy = local(sep_rhs_hbm, sep_rhs, small_sem.at[3])
-    inv_copies = []
-    off_copies = []
-    for j in range(LOC):
-        inv_copies.append(local(inv_hbm.at[j], inv.at[j], inv_sem.at[j]))
-        off_copies.append(local(off_hbm.at[j], off.at[j], off_sem.at[j]))
-
-    sep_inv_copy.wait()
-    coupling_copy.wait()
-    dinv = sep_inv[...]
-    own_v = -times(dinv, coupling[...]).T
-    own_v = jnp.where(s > 0, own_v, 0.0)
-    vpair[core] = own_v
 
     acc[...] = jnp.zeros_like(acc)
     rhs_copy.wait()
 
     def down(j):
-        inv_copies[j].wait()
-        off_copies[j].wait()
+        for copy in tree_copies.get(j, ()):
+            copy.wait()
         y = times_t(rhs[j] - acc[j].reshape(R, W), inv[j])
         ys[j] = y
         products = times_t(y, off[j].reshape(KB * W, W))
@@ -141,34 +134,21 @@
         g_low[j] = low
         given[j] = both[KB * W :]
 
-    for j in range(0, 8):
-        down(j)
-
-    pl.semaphore_wait(barrier, len(greeted))
-    pair_copy = send(vpair.at[core], vpair.at[core], pair_ss, pair_rs, sibling)
-    prev_copy = send(sep_inv, prev_inv, prev_ss, prev_rs, after)
-    for j in range(8, 10):
-        down(j)
-    pair_copy.wait_recv()
-    v0 = vpair[0]
-    v1 = vpair[1]
-    vm = times(v0, v1)
-    vq[m, 0] = vm
-    vq[m, 1] = times_t(v0, v0) + times_t(vm, vm)
     z_copies = {}
-    f_copies = []
+    f_copies = {}
+
+    def chip_at(distance):
+        return lax.rem(m + CHIPS + distance, CHIPS)
 
     def z_send(way, step, piece):
-        source = lax.rem(m + (CHIPS + 1 - step if way == 0 else step - 1), CHIPS)
-        where = vq.at[source, core, pl.ds(piece * (W // 2), W // 2)]
+        source = 2 * chip_at(1 - step if way == 0 else step - 1) + core
+        where = vr.at[source, pl.ds(piece * (W // 2), W // 2)]
         index = way * 8 + (step - 1) * 2 + piece
-        z_copies[way, step, piece] = send(
-            where, where, z_ss.at[index], z_rs.at[index], chip_peer(1 if way == 0 else CHIPS - 1)
-        )
+        z_copies[way, step, piece] = send(where, where, z_ss.at[index], z_rs.at[index], chip_sides[way])
 
     def f_send(distance, index):
-        where = vq.at[lax.rem(m + CHIPS + distance, CHIPS), core]
-        f_copies.append(send(where, where, f_ss.at[index], f_rs.at[index], sibling))
+        where = vr.at[2 * chip_at(distance) + core]
+        f_copies[distance] = send(where, where, f_ss.at[index], f_rs.at[index], sibling)
 
     def z_step(step):
         for piece in range(2):
@@ -179,10 +159,46 @@
         f_send(1 - step, step - 2)
         f_send(step - 1, step + 1)
 
+    def merge(distance):
+        f_copies[distance].wait_recv()
+        chip = chip_at(distance)
+        first, second = vr[2 * chip], vr[2 * chip + 1]
+        pair = times(first, second)
+        vq[chip, 0] = pair
+        vq[chip, 1] = times_t(first, first) + times_t(pair, pair)
+
+    def relay(level, peers):
+        for peer in peers:
+            pl.semaphore_signal(relays.at[level], inc=1, device_id=peer, device_id_type=MESH)
+
+    down(0)
+    sep_inv_copy.wait()
+    coupling_copy.wait()
+    dinv = sep_inv[...]
+    own_v = -times(dinv, coupling[...]).T
+    own_v = jnp.where(s > 0, own_v, 0.0)
+    vr[i] = own_v
+    down(1)
+
+    pl.semaphore_wait(barrier, len(greeted))
     for piece in range(2):
         for way in range(2):
             z_send(way, 1, piece)
-    for j in range(10, LOC):
+    f_send(0, 7)
+    prev_copy = send(sep_inv, prev_inv, prev_ss, prev_rs, after)
+    relay(0, [*chip_sides, plane_peer(3), sub_peer(3)])
+    for j in range(2, 6):
+        down(j)
+    pl.semaphore_wait(relays.at[0], 4)
+    relay(1, chip_sides)
+    for j in range(6, 9):
+        down(j)
+    z_step(2)
+    for j in range(9, 11):
+        down(j)
+    pl.semaphore_wait(relays.at[1], 2)
+    relay(2, chip_sides)
+    for j in range(11, LOC):
         down(j)
 
     red_copies = []
@@ -192,41 +208,45 @@
             send(acc.at[pl.ds(LOC, 2), peer[1]], terms.at[u], red_ss.at[k - 1], red_rs.at[k - 1], peer)
         )
     terms[u] = acc[LOC:, u]
-    z_step(2)
-    for j in range(4):
+    z_step(3)
+    merge(0)
+    v0 = vr[2 * m]
+    v1 = vr[2 * m + 1]
+    vm = vq[m, 0]
+    merge(-1)
+    merge(1)
+    for j in range(0, 4):
         prepare_up(j)
-    z_step(3)
-    for j in range(4, 6):
-        prepare_up(j)
+    pl.semaphore_wait(relays.at[2], 2)
     sep_rhs_copy.wait()
     for copy in red_copies:
         copy.wait_recv()
     prev_copy.wait_recv()
     summed = (terms[0] + terms[1]) + (terms[2] + terms[3])
     delta = jnp.where(s > 0, -times_t(summed[1], prev_inv[...]), 0.0)
-    phi = times_t(sep_rhs[u] - summed[0], dinv) + times(delta, vpair[core])
-    phi_part = jnp.where(first_core, times(phi, v1), phi)
-    part[i, 0] = phi_part
-    part[i, 1] = (
-        times_t(jnp.where(first_core, phi, delta), v0)
-        + jnp.where(first_core, delta, 0.0)
-        + times_t(phi_part, vm)
-    )
+    phi = times_t(sep_rhs[u] - summed[0], dinv) + times(delta, vr[i])
     mine[core, 0] = phi
     mine[core, 1] = delta
+    mine_copy = send(mine.at[core], mine.at[core], mine_ss, mine_rs, sibling)
+    mine_copy.wait_recv()
+    phi_chip = mine[1, 0] + times(mine[0, 0], v1)
+    part[m, 0] = phi_chip
+    part[m, 1] = times_t(mine[0, 0] + mine[1, 1], v0) + mine[0, 1] + times_t(phi_chip, vm)
     ring_copies = []
-    for k in (8, 7, 9, 6, 10, 5, 11, 4, 12, 3, 13, 2, 14, 1, 15):
-        ring_copies.append(send(part.at[i], part.at[i], ring_ss.at[k - 1], ring_rs.at[k - 1], ring_peer(k)))
-    mine_copy = send(mine.at[core], mine.at[core], mine_ss, mine_rs, sibling)
+    for k in far_first:
+        ring_copies.append(send(part.at[m], part.at[m], ring_ss.at[k - 1], ring_rs.at[k - 1], chip_peer(k)))
 
     z_step(4)
-    for j in range(6, 9):
+    merge(-2)
+    merge(2)
+    for j in range(4, 6):
         prepare_up(j)
     z_copies[0, 4, 0].wait_recv()
     z_copies[1, 4, 1].wait_recv()
     f_send(4, 6)
-    for copy in f_copies:
-        copy.wait_recv()
+    merge(-3)
+    merge(3)
+    merge(4)
 
     eye = (
         lax.broadcasted_iota(jnp.int32, (W, W), 0) == lax.broadcasted_iota(jnp.int32, (W, W), 1)
@@ -256,12 +276,11 @@
     for k in (2, 1, 3):
         x_copies.append(send(xg.at[g, core], xg.at[g, core], x_ss.at[k - 1], x_rs.at[k - 1], plane_peer(k)))
 
-    mine_copy.wait_recv()
     for copy in ring_copies:
         copy.wait_recv()
 
-    phis = [part[2 * n, 0] + part[2 * n + 1, 0] for n in range(CHIPS)]
-    xis = [part[2 * n, 1] + part[2 * n + 1, 1] for n in range(CHIPS)]
+    phis = [part[n, 0] for n in range(CHIPS)]
+    xis = [part[n, 1] for n in range(CHIPS)]
     ps, ws, pz = phis[last], xis[last], phis[0]
     suf_w[last] = ws
     pre_z[1] = pz
@@ -287,7 +306,7 @@
         h_copies.append(
             send(xg.at[source, core], xg.at[source, core], h_ss.at[k - 1], h_rs.at[k - 1], sibling)
         )
-    for j in range(9, LOC):
+    for j in range(6, LOC):
         prepare_up(j)
     for copy in h_copies + r_copies:
         copy.wait_recv()
@@ -310,7 +329,7 @@
     z_in = ends[g, 0]
     w_in = ends[g, 1]
     z_chip = pre_z[m] + times(z_in, pre_v[m])
-    z_next = part[2 * m, 0] + part[2 * m + 1, 0] + times(z_chip, vm)
+    z_next = part[m, 0] + times(z_chip, vm)
     w_chip = suf_w[m + 1] + times(z_next, suf_q[m + 1]) + times_t(w_in, suf_v[m + 1])
     z_even = mine[0, 0] + times(z_chip, v0)
     odd = mine[1, 0] + times(z_even, v1) + w_chip
@@ -346,8 +365,8 @@
         learn(j, x)
         x_ref[j] = x
 
-    started = [pair_copy, prev_copy, mine_copy] + list(z_copies.values()) + red_copies + ring_copies + r_copies
-    for copy in started + f_copies + x_copies + h_copies + fin_copies:
+    started = [prev_copy, mine_copy] + list(z_copies.values()) + list(f_copies.values()) + red_copies + ring_copies + r_copies
+    for copy in started + x_copies + h_copies + fin_copies:
         copy.wait_send()
 
 
@@ -393,9 +412,9 @@
             vmem((LOC + 2, SUBS, ROWS, W), F32),
             vmem((LOC, R, W), F32),
             vmem((W, W), F32),
-            vmem((2, W, W), F32),
+            vmem((RING, W, W), F32),
             vmem((CHIPS, 2, W, W), F32),
-            vmem((RING, 2, ROWS, W), F32),
+            vmem((CHIPS, 2, ROWS, W), F32),
             vmem((2, 2, ROWS, W), F32),
             vmem((4, 2, W, W), F32),
             vmem((4, 2, ROWS, W), F32),
@@ -412,12 +431,12 @@
             vmem((LOC, R, W), F32),
             vmem((LOC + 3, R, W), BF),
             vmem((LOC + 3, R, W), BF),
-            dma((LOC,)), dma((LOC,)),
+            dma((5,)), dma((5,)),
             dma(()), dma(()),
-            dma(()), dma(()),
+            pltpu.SemaphoreType.REGULAR((3,)),
             dma((16,)), dma((16,)),
+            dma((8,)), dma((8,)),
             dma((7,)), dma((7,)),
-            dma((15,)), dma((15,)),
             dma(()), dma(()),
             dma((3,)), dma((3,)),
             dma((3,)), dma((3,)),

time: 51.8 us -> 48.3 us (0.932)
  Pallas kernels: 51.1 us -> 47.5 us
    pallas_call x1, Pallas kernels: 49.4 us -> 45.8 us  [shards(): pl.pallas_call(solve_kernel, name='solve', out_shape=(rows_of(LOC, R, W),...]
where the time goes in v3:
time: 48.3 us; the launch traced here: 48.2 us
  Pallas kernels  47.5 us (98%)
  between operations  0.64 us (1%)
    pallas_call x1, Pallas kernels, shards(): pl.pallas_call(solve_kernel, name='solve', out_shape=(rows_of(LOC, R, W),...  45.8 us
    pallas_call x1, Pallas kernels, shards(): pl.pallas_call(store_kernel, name='store', out_shape=(rows_of(LOC, R, W),...  1.67 us

profile of v3, /device:TPU:1, one launch (start us, length us, event | category | flops | bytes accessed | tf_op | source)
XLA Modules:
  0.0 48.2 jit_solution(18366921313005948062)
XLA Ops:
  0.6 45.8 %solve.1 = (f32[16,32,128]{2,1,0:T(8,128)}, f32[32,128]{1,0:T(8,128)}) custom-call(s32[4,16]{1,0:T(4,128)} %bitcast.17, f32[16,32,128]{2,1,0:T(8,128)} %bitcast.13, f32[16,128,128]{2,1,0:T(8,128)} %bitcast.12, f32[16,4,128,128]{3,2,1,0:T(8,128)} %bitcast.11, f32[4,8,128]{2,1,0:T(8,128)} %bitcast.16, f32[128,128]{1,0:T(8,128)} %bitcast.14, f32[128,128]{1,0:T(8,128)} %bitcast.15), custom_call_target="tpu_custom_call" | custom-call | tf_op jit(solution)/shard_map/solve/pallas_call | solution.py:398
  46.5 1.7 %store.1 = (f32[16,32,128]{2,1,0:T(8,128)}, f32[32,128]{1,0:T(8,128)}) custom-call(f32[16,32,128]{2,1,0:T(8,128)} %get-tuple-element.6.x, f32[32,128]{1,0:T(8,128)} %get-tuple-element.7.own), custom_call_target="tpu_custom_call" | custom-call | tf_op jit(solution)/shard_map/store/pallas_call | solution.py:451

commit v4 on v3

--- a/solution.py
+++ b/solution.py
@@ -218,6 +218,7 @@
     for j in range(0, 4):
         prepare_up(j)
     pl.semaphore_wait(relays.at[2], 2)
+    z_step(4)
     sep_rhs_copy.wait()
     for copy in red_copies:
         copy.wait_recv()
@@ -236,7 +237,6 @@
     for k in far_first:
         ring_copies.append(send(part.at[m], part.at[m], ring_ss.at[k - 1], ring_rs.at[k - 1], chip_peer(k)))
 
-    z_step(4)
     merge(-2)
     merge(2)
     for j in range(4, 6):

time: 48.3 us -> 46.6 us (0.965)
  Pallas kernels: 47.5 us -> 45.9 us
    pallas_call x1, Pallas kernels: 45.8 us -> 44.2 us  [shards(): pl.pallas_call(solve_kernel, name='solve', out_shape=(rows_of(LOC, R, W),...]
where the time goes in v4:
time: 46.6 us; the launch traced here: 46.5 us
  Pallas kernels  45.9 us (98%)
  between operations  0.64 us (1%)
    pallas_call x1, Pallas kernels, shards(): pl.pallas_call(solve_kernel, name='solve', out_shape=(rows_of(LOC, R, W),...  44.2 us
    pallas_call x1, Pallas kernels, shards(): pl.pallas_call(store_kernel, name='store', out_shape=(rows_of(LOC, R, W),...  1.67 us

profile of v4, /device:TPU:1, one launch (start us, length us, event | category | flops | bytes accessed | tf_op | source)
XLA Modules:
  0.0 46.5 jit_solution(7260972337687452167)
XLA Ops:
  0.6 44.2 %solve.1 = (f32[16,32,128]{2,1,0:T(8,128)}, f32[32,128]{1,0:T(8,128)}) custom-call(s32[4,16]{1,0:T(4,128)} %bitcast.17, f32[16,32,128]{2,1,0:T(8,128)} %bitcast.13, f32[16,128,128]{2,1,0:T(8,128)} %bitcast.12, f32[16,4,128,128]{3,2,1,0:T(8,128)} %bitcast.11, f32[4,8,128]{2,1,0:T(8,128)} %bitcast.16, f32[128,128]{1,0:T(8,128)} %bitcast.14, f32[128,128]{1,0:T(8,128)} %bitcast.15), custom_call_target="tpu_custom_call" | custom-call | tf_op jit(solution)/shard_map/solve/pallas_call | solution.py:398
  44.8 1.7 %store.1 = (f32[16,32,128]{2,1,0:T(8,128)}, f32[32,128]{1,0:T(8,128)}) custom-call(f32[16,32,128]{2,1,0:T(8,128)} %get-tuple-element.6.x, f32[32,128]{1,0:T(8,128)} %get-tuple-element.7.own), custom_call_target="tpu_custom_call" | custom-call | tf_op jit(solution)/shard_map/store/pallas_call | solution.py:451

commit v5 on v4

--- a/solution.py
+++ b/solution.py
@@ -256,12 +256,26 @@
     suf_w[CHIPS] = jnp.zeros((ROWS, W), F32)
     pre_v[0] = eye
     pre_z[0] = jnp.zeros((ROWS, W), F32)
+    level = [(vq[n, 0], vq[n, 1]) for n in range(CHIPS)]
+    while len(level) > 1:
+        merged = []
+        for (va, qa), (vb, qb) in zip(level[::2], level[1::2]):
+            both = times(va, jnp.concatenate([vb, qb], 1))
+            merged.append((both[:, :W], qa + times_t(both[:, W:], va)))
+        level = merged
+    vs, qs = level[0]
+    xg[g, 0] = vs
+    xg[g, 1] = qs
+    x_copies = []
+    for k in (2, 1, 3):
+        x_copies.append(send(xg.at[g, core], xg.at[g, core], x_ss.at[k - 1], x_rs.at[k - 1], plane_peer(k)))
+
     last = CHIPS - 1
     vs, qs = vq[last, 0], vq[last, 1]
     suf_v[last], suf_q[last] = vs, qs
     pv = vq[0, 0]
     pre_v[1] = pv
-    for n in reversed(range(last)):
+    for n in reversed(range(1, last)):
         both = times(vq[n, 0], jnp.concatenate([vs, qs], 1))
         vs = both[:, :W]
         qs = vq[n, 1] + times_t(both[:, W:], vq[n, 0])
@@ -270,12 +284,6 @@
         if up < last:
             pv = times(pv, vq[up, 0])
             pre_v[up + 1] = pv
-    xg[g, 0] = vs
-    xg[g, 1] = qs
-    x_copies = []
-    for k in (2, 1, 3):
-        x_copies.append(send(xg.at[g, core], xg.at[g, core], x_ss.at[k - 1], x_rs.at[k - 1], plane_peer(k)))
-
     for copy in ring_copies:
         copy.wait_recv()
 

time: 46.6 us -> 45.3 us (0.972)
  Pallas kernels: 45.9 us -> 44.5 us
    pallas_call x1, Pallas kernels: 44.2 us -> 42.9 us  [shards(): pl.pallas_call(solve_kernel, name='solve', out_shape=(rows_of(LOC, R, W),...]
where the time goes in v5:
time: 45.3 us; the launch traced here: 45.2 us
  Pallas kernels  44.5 us (98%)
  between operations  0.64 us (1%)
    pallas_call x1, Pallas kernels, shards(): pl.pallas_call(solve_kernel, name='solve', out_shape=(rows_of(LOC, R, W),...  42.9 us
    pallas_call x1, Pallas kernels, shards(): pl.pallas_call(store_kernel, name='store', out_shape=(rows_of(LOC, R, W),...  1.67 us

profile of v5, /device:TPU:1, one launch (start us, length us, event | category | flops | bytes accessed | tf_op | source)
XLA Modules:
  0.0 45.2 jit_solution(7728266379174231064)
XLA Ops:
  0.6 42.9 %solve.1 = (f32[16,32,128]{2,1,0:T(8,128)}, f32[32,128]{1,0:T(8,128)}) custom-call(s32[4,16]{1,0:T(4,128)} %bitcast.17, f32[16,32,128]{2,1,0:T(8,128)} %bitcast.13, f32[16,128,128]{2,1,0:T(8,128)} %bitcast.12, f32[16,4,128,128]{3,2,1,0:T(8,128)} %bitcast.11, f32[4,8,128]{2,1,0:T(8,128)} %bitcast.16, f32[128,128]{1,0:T(8,128)} %bitcast.14, f32[128,128]{1,0:T(8,128)} %bitcast.15), custom_call_target="tpu_custom_call" | custom-call | tf_op jit(solution)/shard_map/solve/pallas_call | solution.py:406
  43.5 1.7 %store.1 = (f32[16,32,128]{2,1,0:T(8,128)}, f32[32,128]{1,0:T(8,128)}) custom-call(f32[16,32,128]{2,1,0:T(8,128)} %get-tuple-element.6.x, f32[32,128]{1,0:T(8,128)} %get-tuple-element.7.own), custom_call_target="tpu_custom_call" | custom-call | tf_op jit(solution)/shard_map/store/pallas_call | solution.py:459

commit v6 on v5

--- a/solution.py
+++ b/solution.py
@@ -185,7 +185,6 @@
         for way in range(2):
             z_send(way, 1, piece)
     f_send(0, 7)
-    prev_copy = send(sep_inv, prev_inv, prev_ss, prev_rs, after)
     relay(0, [*chip_sides, plane_peer(3), sub_peer(3)])
     for j in range(2, 6):
         down(j)
@@ -194,6 +193,7 @@
     for j in range(6, 9):
         down(j)
     z_step(2)
+    prev_copy = send(sep_inv, prev_inv, prev_ss, prev_rs, after)
     for j in range(9, 11):
         down(j)
     pl.semaphore_wait(relays.at[1], 2)

time: 45.3 us -> 44.7 us (0.987)
  Pallas kernels: 44.5 us -> 44 us
    pallas_call x1, Pallas kernels: 42.9 us -> 42.3 us  [shards(): pl.pallas_call(solve_kernel, name='solve', out_shape=(rows_of(LOC, R, W),...]
where the time goes in v6:
time: 44.7 us; the launch traced here: 44.6 us
  Pallas kernels  44 us (98%)
  between operations  0.64 us (1%)
    pallas_call x1, Pallas kernels, shards(): pl.pallas_call(solve_kernel, name='solve', out_shape=(rows_of(LOC, R, W),...  42.3 us
    pallas_call x1, Pallas kernels, shards(): pl.pallas_call(store_kernel, name='store', out_shape=(rows_of(LOC, R, W),...  1.67 us

profile of v6, /device:TPU:1, one launch (start us, length us, event | category | flops | bytes accessed | tf_op | source)
XLA Modules:
  0.0 44.6 jit_solution(17183348477285367699)
XLA Ops:
  0.6 42.3 %solve.1 = (f32[16,32,128]{2,1,0:T(8,128)}, f32[32,128]{1,0:T(8,128)}) custom-call(s32[4,16]{1,0:T(4,128)} %bitcast.17, f32[16,32,128]{2,1,0:T(8,128)} %bitcast.13, f32[16,128,128]{2,1,0:T(8,128)} %bitcast.12, f32[16,4,128,128]{3,2,1,0:T(8,128)} %bitcast.11, f32[4,8,128]{2,1,0:T(8,128)} %bitcast.16, f32[128,128]{1,0:T(8,128)} %bitcast.14, f32[128,128]{1,0:T(8,128)} %bitcast.15), custom_call_target="tpu_custom_call" | custom-call | tf_op jit(solution)/shard_map/solve/pallas_call | solution.py:406
  42.9 1.7 %store.1 = (f32[16,32,128]{2,1,0:T(8,128)}, f32[32,128]{1,0:T(8,128)}) custom-call(f32[16,32,128]{2,1,0:T(8,128)} %get-tuple-element.6.x, f32[32,128]{1,0:T(8,128)} %get-tuple-element.7.own), custom_call_target="tpu_custom_call" | custom-call | tf_op jit(solution)/shard_map/store/pallas_call | solution.py:459
